TPU v7x, 256 devices: a whole 4x4x8 slice. The times are simulated.
256 devices in a mesh: frame: 8 (over z_hi, core), slab: 32 (over z_lo, x, y).
Axes of the slice: x: 4, y: 4, z: 8 (z_hi: 4, z_lo: 2; z = z_hi * 2 + z_lo), core: 2. Of those that a mesh axis runs over, the one named last changes fastest.
Arguments:
- volume: float32 [8, 1024, 16384], P('frame', 'slab'), may hold values from -6 to 6
- measured: float32 [8, 2, 1024, 16384], P('frame', None, None, 'slab'), may hold values from -6 to 6
- cutoff: int32 [8, 16384], P('frame', 'slab'), may hold values from 128 to 384
Outputs:
- smoothed: float32 [8, 1024, 16384], P('frame', 'slab')
All inputs are finite; a program needn't handle non-finite values.
Results may differ from a plain program's by a relative error of at most 0.0003.
Values sent between devices are 32-bit elements; how exact they have to be, the bound alone decides.
A program may use at most 128 MiB of HBM per device.

v0:
```python
import math

import jax
import jax.numpy as jnp
from jax import lax
from jax.sharding import PartitionSpec as P

tv_step_size = 0.25
tv_weight = 1.0


def extended_2(block, sides, width):
    for axis, dim in sides:
        count = lax.axis_size(axis)
        forward = [(i, i + 1) for i in range(count - 1)]
        backward = [(target, source) for source, target in forward]
        low = lax.ppermute(
            lax.slice_in_dim(block, block.shape[dim] - width, None, axis=dim), axis, forward
        )
        high = lax.ppermute(lax.slice_in_dim(block, 0, width, axis=dim), axis, backward)
        block = jnp.concatenate([low, block, high], axis=dim)
    return block


def tv_step(extended, anchor, first_frame, frames):
    difference = extended[1:] - extended[:-1]
    frame_ids = first_frame + jnp.arange(difference.shape[0], dtype=jnp.int32)
    inside = ((frame_ids >= 0) & (frame_ids <= frames - 2))[:, None, None]
    fluxes = jnp.where(inside, difference / jnp.sqrt(difference * difference + 1.0), 0.0)
    interior = extended[1:-1]
    return interior - tv_step_size * (interior - anchor + tv_weight * (fluxes[:-1] - fluxes[1:]))


def tables(length):
    indices = jnp.arange(length, dtype=jnp.int32)
    product = indices[:, None] * indices[None, :] % length
    angle = product.astype(jnp.float32) * (2.0 * math.pi / length)
    scale = 1.0 / math.sqrt(length)
    return (jnp.cos(angle) * scale, jnp.sin(angle) * scale)


def back_to_slabs(columns):
    return lax.all_to_all(columns, "slab", split_axis=1, concat_axis=2, tiled=True)


def smooth(anchor, first_frame, frames):
    current = anchor
    for step in range(2):
        extended = extended_2(current, (("frame", 0),), 1)
        current = tv_step(extended, anchor, first_frame - 1, frames)
    return current


def on_device(volume, measured, cutoff):
    columns = lax.all_to_all(volume, "slab", split_axis=2, concat_axis=1, tiled=True)
    length = columns.shape[1]
    cos_table, sin_table = tables(length)
    highest = lax.Precision.HIGHEST
    local_frames = columns.shape[0]
    frames = lax.axis_size("frame") * local_frames
    first_frame = lax.axis_index("frame") * local_frames
    indices = jnp.arange(length, dtype=jnp.int32)
    signed = jnp.where(indices < length // 2, indices, indices - length)
    column_field = columns[0]
    real_part = jnp.dot(
        cos_table, column_field, precision=highest, preferred_element_type=jnp.float32
    )
    imag_part = -jnp.dot(
        sin_table, column_field, precision=highest, preferred_element_type=jnp.float32
    )
    measured_mask = jnp.abs(signed)[:, None] <= cutoff[0][None, :]
    real_part = jnp.where(measured_mask, measured[0, 0], real_part)
    imag_part = jnp.where(measured_mask, measured[0, 1], imag_part)
    restored = jnp.dot(cos_table, real_part, precision=highest, preferred_element_type=jnp.float32)
    restored = restored - jnp.dot(
        sin_table, imag_part, precision=highest, preferred_element_type=jnp.float32
    )
    restored_list = [restored]
    anchor = jnp.stack(restored_list, axis=0)
    slabs = back_to_slabs(anchor)
    return smooth(slabs, first_frame, frames)


def solution(mesh):
    placed = (P("frame", "slab", None), P("frame", None, None, "slab"), P("frame", "slab"))
    return jax.shard_map(
        on_device, mesh=mesh, in_specs=placed, out_specs=P("frame", "slab", None), check_vma=False
    )
```

profile of v0, /device:TPU:65, one launch (start us, length us, event | category | flops | bytes accessed | tf_op | source)
XLA Modules:
  0.0 409.7 jit_solution(1470449793287851825)
XLA Ops:
  0.0 16.7 %copy.8 = f32[1,32,16384]{1,0,2:T(1,128)} copy(f32[1,32,16384]{2,1,0:T(8,128)} %param.3) | data formatting | bytes 4194304 | tf_op args[0]
  16.7 0.5 broadcast.91
  17.2 74.5 %reduce = f32[16384,32]{1,0:T(8,128)} reduce(f32[16384,1,32]{2,1,0:T(1,128)} %bitcast.27, f32[]{:T(128)} %broadcast.91), dimensions={1}, to_apply=%bitcast.23.reduce_sub_computation | reduce | bytes 4194308
  91.7 7.7 %reshape.29 = f32[32,1,16384]{2,1,0:T(1,128)} reshape(f32[16384,32]{1,0:T(8,128)} %reduce) | data formatting | bytes 4194304
  99.4 8.7 %all-to-all-start = ((f32[32,1,16384]{2,1,0:T(1,128)}), f32[32,1,16384]{2,1,0:T(1,128)}, u32[]{:S(2)}, u32[]{:S(2)}) async-start(f32[32,1,16384]{2,1,0:T(1,128)} %reshape.29), calls=%async_computation | async-start | bytes 4194304 | tf_op jit(solution)/shard_map/all_to_all | solution.py:55
  108.2 25.6 %all-to-all-done = f32[32,1,16384]{2,1,0:T(1,128)} async-done(((f32[32,1,16384]{2,1,0:T(1,128)}), f32[32,1,16384]{2,1,0:T(1,128)}, u32[]{:S(2)}, u32[]{:S(2)}) %all-to-all-start) | async-done | bytes 2097184 | tf_op jit(solution)/shard_map/all_to_all | solution.py:55
  133.8 7.4 %reduce.1 = f32[32,16384]{1,0:T(8,128)S(1)} reduce(f32[32,1,16384]{2,1,0:T(1,128)} %all-to-all-done, f32[]{:T(128)} %broadcast.91), dimensions={1}, to_apply=%all_to_all.24.reduce_sub_computation | reduce | bytes 4194308 | tf_op jit(solution)/shard_map/all_to_all | solution.py:55
  141.2 15.4 %reshape.30 = f32[16384,1,32]{2,1,0:T(1,128)} reshape(f32[32,16384]{1,0:T(8,128)S(1)} %reduce.1) | data formatting | bytes 4194304
  156.6 5.9 %copy.13 = f32[1,32,32,512]{3,2,1,0:T(8,128)S(1)} copy(f32[1,32,32,512]{1,3,2,0:T(8,128)} %bitcast.28) | data formatting | bytes 4194304 | tf_op jit(solution)/shard_map/all_to_all | solution.py:55
  162.5 1.2 copy.10
  163.7 22.2 %fusion.7 = f32[1024,512]{1,0:T(8,128)S(1)} fusion(f32[1024,512]{1,0:T(8,128)S(1)} %bitcast.31), kind=kOutput, calls=%fused_computation.16 | convolution fusion | flops 6458179584 | bytes 4194304 | tf_op jit(solution)/shard_map/dot_general | solution.py:65
  185.9 0.0 copy-start
  185.9 0.0 copy-start.1
  185.9 22.8 %fusion.9 = f32[1024,512]{1,0:T(8,128)S(1)} fusion(f32[1024,512]{1,0:T(8,128)S(1)} %bitcast.32), kind=kOutput, calls=%fused_computation.18 | convolution fusion | flops 6458179584 | bytes 4194304 | tf_op jit(solution)/shard_map/dot_general | solution.py:68
  208.7 0.0 copy-done
  208.7 0.0 copy-done.1
  208.7 22.7 %fusion.6 = f32[1024,512]{1,0:T(8,128)S(1)} fusion(f32[1024,512]{1,0:T(8,128)S(1)} %fusion.7, f32[1,2,1024,512]{3,2,1,0:T(8,128)S(1)} %copy-done, s32[512]{0:T(512)S(1)} %bitcast.33, s32[1024]{0:T(1024)S(1)} %fusion.33), kind=kOutput, calls=%fused_computation.15 | convolution fusion | flops 6459228160 | bytes 6297600 | tf_op jit(solution)/shard_map/dot_general | solution.py:74
  231.4 23.6 %subtract_bitcast_fusion = f32[1,1024,512]{2,1,0:T(8,128)S(1)} fusion(f32[1024,512]{1,0:T(8,128)S(1)} %fusion.6, f32[1024,512]{1,0:T(8,128)S(1)} %fusion.9, f32[1,2,1024,512]{3,2,1,0:T(8,128)S(1)} %copy-done, s32[512]{0:T(512)S(1)} %bitcast.34, s32[1024]{0:T(1024)S(1)} %fusion.33), kind=kOutput, calls=%fused_computation.31 | convolution fusion | flops 6460276736 | bytes 8394752 | tf_op jit(solution)/shard_map/dot_general | solution.py:75
  255.0 2.2 copy.11
  257.1 33.5 %all_to_all.33 = f32[1,1024,512]{2,0,1:T(1,128)S(1)} all-to-all(f32[1,1024,512]{2,0,1:T(1,128)S(1)} %copy.11), channel_id=1, replica_groups=mesh['frame'=8,'slab'=32] {'slab'}, dimensions={1} | all-to-all | bytes 4194304 | tf_op jit(solution)/shard_map/all_to_all | solution.py:43
  290.6 2.5 copy.12
  293.2 1.7 all_to_all.30
  294.9 4.2 %collective-permute-start = (f32[1,32,16384]{2,1,0:T(8,128)S(1)}, f32[1,32,16384]{2,1,0:T(8,128)}, u32[]{:S(2)}, u32[]{:S(2)}) collective-permute-start(f32[1,32,16384]{2,1,0:T(8,128)S(1)} %all_to_all.30), channel_id=1, source_target_pairs={{32,0},{64,32},{96,64},{128,96},{160,128},{192,160},{224,192},{33,... | collective-permute-start | bytes 6291464 | tf_op jit(solution)/shard_map/ppermute | solution.py:20
  299.2 5.1 %collective-permute-start.1 = (f32[1,32,16384]{2,1,0:T(8,128)S(1)}, f32[1,32,16384]{2,1,0:T(8,128)}, u32[]{:S(2)}, u32[]{:S(2)}) collective-permute-start(f32[1,32,16384]{2,1,0:T(8,128)S(1)} %all_to_all.30), channel_id=1, source_target_pairs={{0,32},{32,64},{64,96},{96,128},{128,160},{160,192},{192,224},{1,3... | collective-permute-start | bytes 6291464 | tf_op jit(solution)/shard_map/ppermute | solution.py:17
  304.3 44.3 %collective-permute-done = f32[1,32,16384]{2,1,0:T(8,128)} collective-permute-done((f32[1,32,16384]{2,1,0:T(8,128)S(1)}, f32[1,32,16384]{2,1,0:T(8,128)}, u32[]{:S(2)}, u32[]{:S(2)}) %collective-permute-start) | collective-permute-done | bytes 2097184 | tf_op jit(solution)/shard_map/ppermute | solution.py:20
  348.6 1.0 collective-permute-done.1
  349.7 2.6 multiply_select_fusion.1
  352.3 0.3 fusion.15
  352.6 1.9 collective-permute-start.2
  354.6 6.7 %collective-permute-start.3 = (f32[1,32,16384]{2,1,0:T(8,128)S(1)}, f32[1,32,16384]{2,1,0:T(8,128)S(1)}, u32[]{:S(2)}, u32[]{:S(2)}) collective-permute-start(f32[1,32,16384]{2,1,0:T(8,128)S(1)} %fusion.15), channel_id=1, source_target_pairs={{0,32},{32,64},{64,96},{96,128},{128,160},{160,192},{192,224},{1,3... | collective-permute-start | bytes 6291464 | tf_op jit(solution)/shard_map/ppermute | solution.py:17
  361.2 44.2 %collective-permute-done.2 = f32[1,32,16384]{2,1,0:T(8,128)S(1)} collective-permute-done((f32[1,32,16384]{2,1,0:T(8,128)S(1)}, f32[1,32,16384]{2,1,0:T(8,128)S(1)}, u32[]{:S(2)}, u32[]{:S(2)}) %collective-permute-start.2) | collective-permute-done | bytes 2097184 | tf_op jit(solution)/shard_map/ppermute | solution.py:20
  405.5 1.1 collective-permute-done.3
  406.6 0.9 multiply_select_fusion
  407.5 1.8 fusion.12
  (2 shorter events, 0.0 us)
Async XLA Ops:
  99.4 34.4 %all-to-all-start = ((f32[32,1,16384]{2,1,0:T(1,128)}), f32[32,1,16384]{2,1,0:T(1,128)}, u32[]{:S(2)}, u32[]{:S(2)}) async-start(f32[32,1,16384]{2,1,0:T(1,128)} %reshape.29), calls=%async_computation | async-start | bytes 4194304 | tf_op jit(solution)/shard_map/all_to_all | solution.py:55
  185.9 22.8 %copy-start = (f32[1,2,1024,512]{3,2,1,0:T(8,128)S(1)}, f32[1,2,1024,512]{3,2,1,0:T(8,128)}, u32[]{:S(2)}) copy-start(f32[1,2,1024,512]{3,2,1,0:T(8,128)} %param.4) | copy-start | bytes 12582916
  185.9 22.8 %copy-start.1 = (s32[1,512]{1,0:T(1,128)S(1)}, s32[1,512]{1,0:T(1,128)}, u32[]{:S(2)}) copy-start(s32[1,512]{1,0:T(1,128)} %param.5) | copy-start | bytes 6148
  294.9 53.7 %collective-permute-start = (f32[1,32,16384]{2,1,0:T(8,128)S(1)}, f32[1,32,16384]{2,1,0:T(8,128)}, u32[]{:S(2)}, u32[]{:S(2)}) collective-permute-start(f32[1,32,16384]{2,1,0:T(8,128)S(1)} %all_to_all.30), channel_id=1, source_target_pairs={{32,0},{64,32},{96,64},{128,96},{160,128},{192,160},{224,192},{33,... | collective-permute-start | bytes 6291464 | tf_op jit(solution)/shard_map/ppermute | solution.py:20
  299.2 50.5 %collective-permute-start.1 = (f32[1,32,16384]{2,1,0:T(8,128)S(1)}, f32[1,32,16384]{2,1,0:T(8,128)}, u32[]{:S(2)}, u32[]{:S(2)}) collective-permute-start(f32[1,32,16384]{2,1,0:T(8,128)S(1)} %all_to_all.30), channel_id=1, source_target_pairs={{0,32},{32,64},{64,96},{96,128},{128,160},{160,192},{192,224},{1,3... | collective-permute-start | bytes 6291464 | tf_op jit(solution)/shard_map/ppermute | solution.py:17
  352.6 52.8 %collective-permute-start.2 = (f32[1,32,16384]{2,1,0:T(8,128)S(1)}, f32[1,32,16384]{2,1,0:T(8,128)S(1)}, u32[]{:S(2)}, u32[]{:S(2)}) collective-permute-start(f32[1,32,16384]{2,1,0:T(8,128)S(1)} %fusion.15), channel_id=1, source_target_pairs={{32,0},{64,32},{96,64},{128,96},{160,128},{192,160},{224,192},{33,... | collective-permute-start | bytes 6291464 | tf_op jit(solution)/shard_map/ppermute | solution.py:20
  354.6 52.0 %collective-permute-start.3 = (f32[1,32,16384]{2,1,0:T(8,128)S(1)}, f32[1,32,16384]{2,1,0:T(8,128)S(1)}, u32[]{:S(2)}, u32[]{:S(2)}) collective-permute-start(f32[1,32,16384]{2,1,0:T(8,128)S(1)} %fusion.15), channel_id=1, source_target_pairs={{0,32},{32,64},{64,96},{96,128},{128,160},{160,192},{192,224},{1,3... | collective-permute-start | bytes 6291464 | tf_op jit(solution)/shard_map/ppermute | solution.py:17
where the time goes:
time: 415 us; the launch traced here: 410 us
  waiting for transfers between devices  116 us (28%)
  matrix products  91.2 us (22%)
  other arithmetic  87.5 us (21%)
  local copies, waits for them, and re-layouts  53.9 us (13%)
  blocking collectives  33.5 us (8%)
  starting transfers between devices  26.7 us (6%)
    ppermute x2, waiting for transfers between devices, extended_2(): lax.ppermute(lax.slice_in_dim(block, 0, width, axis=dim), axis, backward)  88.6 us
    unnamed x1, other arithmetic  74.5 us
    unnamed x8, local copies, waits for them, and re-layouts  40.4 us
    all_to_all x1, blocking collectives, back_to_slabs(): lax.all_to_all(columns, 'slab', split_axis=1, concat_axis=2, tiled=True)  33.5 us
    all_to_all x1, waiting for transfers between devices, on_device(): lax.all_to_all(volume, 'slab', split_axis=2, concat_axis=1, tiled=True)  25.6 us
    dot_general x1, matrix products, on_device(): jnp.dot(sin_table, imag_part, precision=highest, preferred_element_type=j...  23.6 us
    dot_general x1, matrix products, on_device(): jnp.dot(sin_table, column_field, precision=highest, preferred_element_typ...  22.8 us
    dot_general x1, matrix products, on_device(): jnp.dot(cos_table, real_part, precision=highest, preferred_element_type=j...  22.7 us
  transfers between devices with their start and end apart: 5, of which 5 were waited for; matrix products, arithmetic and copies ran while one was open for 0% of the time, Pallas kernels for 0%

commit v1 on v0

v1 whole, which is shorter than its diff:
```python
import functools

import jax
import jax.numpy as jnp
import ml_dtypes
import numpy as np
from jax import lax
from jax.experimental import pallas as pl
from jax.experimental.pallas import tpu as pltpu
from jax.sharding import PartitionSpec as P

MESH = pl.DeviceIdType.MESH
F32, BF16 = jnp.float32, jnp.bfloat16
step_size = 0.25
tv_weight = 1.0


def tables(length):
    index = np.arange(length, dtype=np.int64)
    angle = (index[:, None] * index[None, :] % length) * (2.0 * np.pi / length)
    parts = []
    for table in (np.cos(angle), -np.sin(angle)):
        table = table / np.sqrt(length)
        head = table.astype(ml_dtypes.bfloat16)
        rest = (table - head.astype(np.float64)).astype(ml_dtypes.bfloat16)
        parts += [head, rest]
    return parts


def flux(d):
    return d * lax.rsqrt(d * d + 1.0)


def split(x):
    head = x.astype(BF16)
    rest = (x - head.astype(F32)).astype(BF16)
    return head, rest


def kernel(
    cfg,
    volume, measured, cutoff, ch_hbm, cl_hbm, sh_hbm, sl_hbm,
    out,
    cols, anchor_cols, meas, ch, cl, sh, sl, rhs, rhs2,
    slab, halo, part, own1, near1, part1,
    local_sem, meas_sem, f_send, f_recv, b_send, b_recv, h_send, h_recv, p_send, p_recv, q_send, q_recv,
):
    length, slabs, rows, width, n, chunks, kr, kp, kranges = cfg
    half = slabs // 2
    frame, me = lax.axis_index("frame"), lax.axis_index("slab")
    frames = lax.axis_size("frame")
    block, core = lax.div(frame, 2), lax.rem(frame, 2)
    blocks = frames // 2
    z_lo, place = lax.div(me, half), lax.rem(me, half)
    partner = frame + 1 - 2 * core
    full_frame = jnp.where(z_lo == 1, 2 * block + 2, 2 * block - 1)
    full_there = jnp.where(z_lo == 1, block < blocks - 1, block > 0)
    half_frame = jnp.where(z_lo == 1, 2 * block - 1, 2 * block + 2)
    half_there = jnp.where(z_lo == 1, block > 0, block < blocks - 1)
    near_block = jnp.where(core == 0, block - 1, block + 1)
    near_there = jnp.where(core == 0, block > 0, block < blocks - 1)

    def send(src, dst, send_sem, recv_sem, to_frame, to_slab):
        pltpu.make_async_remote_copy(
            src_ref=src, dst_ref=dst, send_sem=send_sem, recv_sem=recv_sem,
            device_id=(to_frame, to_slab), device_id_type=MESH,
        ).start()

    def wait(like, sem):
        pltpu.make_async_copy(like, like, sem).wait()

    def peer_of(step, across):
        if half == 16:
            there = lax.rem(lax.div(place, 4) + lax.div(step, 4), 4) * 4 + lax.rem(place + step, 4)
        else:
            there = lax.rem(place + step, half)
        return (1 - z_lo if across else z_lo) * half + there

    local = [
        pltpu.make_async_copy(src, dst, local_sem.at[i])
        for i, (src, dst) in enumerate(((ch_hbm, ch), (cl_hbm, cl), (sh_hbm, sh), (sl_hbm, sl)))
    ]
    local += [
        pltpu.make_async_copy(measured.at[0, :, :, pl.ds(c * n, n)], meas.at[c], meas_sem.at[c])
        for c in range(chunks)
    ]
    for copy in local:
        copy.start()

    barrier = pltpu.get_barrier_semaphore()

    def greet(to_frame, to_slab):
        pl.semaphore_signal(barrier, inc=1, device_id=(to_frame, to_slab), device_id_type=MESH)

    @pl.loop(0, half)
    def _(step):
        greet(frame, peer_of(step, True))

        @pl.when(step > 0)
        def _():
            greet(frame, peer_of(step, False))

        @pl.when(near_there & (z_lo == core))
        def _():
            greet(2 * near_block, peer_of(step, True))
            greet(2 * near_block + 1, peer_of(step, True))

    greet(partner, me)

    @pl.when(near_there)
    def _():
        greet(2 * near_block, me)
        greet(2 * near_block + 1, me)

    expected = (
        slabs
        + jnp.where(full_there, half + 1, 0)
        + jnp.where(half_there, 1, 0)
    )
    pl.semaphore_wait(barrier, expected)

    @pl.loop(0, chunks)
    def _(c):
        def source(peer):
            return volume.at[0, :, pl.ds(pl.multiple_of(peer * width + c * n, n), n)]

        target = cols.at[c, pl.ds(pl.multiple_of(me * rows, rows), rows), :]

        @pl.loop(0, half)
        def _(step):
            peer = peer_of(step, True)
            send(source(peer), target, f_send.at[c], f_recv.at[c], frame, peer)

            @pl.when(step > 0)
            def _():
                peer = peer_of(step, False)
                send(source(peer), target, f_send.at[c], f_recv.at[c], frame, peer)

        pltpu.make_async_copy(source(me), target, f_recv.at[c]).start()

    for copy in local[:4]:
        copy.wait()

    if kp > kr:
        rhs2[:, kr:, :] = jnp.zeros((2, kp - kr, 2 * n), BF16)
    tile = min(256, length)
    tiles = length // tile

    def product(at, ranges, right):
        wide, narrow = None, None
        for half_index, (head, rest) in enumerate(((ch, cl), (sh, sl))):
            for low, high, base in ranges:
                both = right[half_index, base : base + high - low, :]
                first = jnp.dot(head[at, low:high], both, preferred_element_type=F32)
                second = jnp.dot(rest[at, low:high], both[:, :n], preferred_element_type=F32)
                wide = first if wide is None else wide + first
                narrow = second if narrow is None else narrow + second
        return wide[:, :n] + wide[:, n:] + narrow

    def transform(c):
        limit = cutoff[0:1, pl.ds(pl.multiple_of(c * n, n), n)]
        wait(meas.at[c], meas_sem.at[c])
        for low, high, base in kranges:
            k = lax.broadcasted_iota(jnp.int32, (high - low, n), 0) + low
            inside = jnp.minimum(k, length - k) <= limit
            for i in range(2):
                head, rest = split(jnp.where(inside, meas[c, i, low:high, :], 0.0))
                rhs[i, base : base + high - low, :n] = head
                rhs[i, base : base + high - low, n:] = rest

        @pl.loop(0, tiles)
        def _(t):
            at = pl.ds(pl.multiple_of(t * tile, tile), tile)
            anchor_cols[c, at, :] = product(at, kranges, rhs)

        wait(cols.at[c], f_recv.at[c])
        head, rest = split(cols[c])
        rhs[0, 0:length, :n] = head
        rhs[0, 0:length, n:] = rest
        k = lax.broadcasted_iota(jnp.int32, (kr, n), 0)
        weight = jnp.where(k <= limit, jnp.where(k == 0, 1.0, 2.0), 0.0)
        for i, (head, rest) in enumerate(((ch, cl), (sh, sl))):
            both = rhs[0, 0:length, :]
            wide = jnp.dot(head[:kr, :], both, preferred_element_type=F32)
            narrow = jnp.dot(rest[:kr, :], both[:, :n], preferred_element_type=F32)
            first, second = split((wide[:, :n] + wide[:, n:] + narrow) * weight)
            rhs2[i, :kr, :n] = first
            rhs2[i, :kr, n:] = second

        @pl.loop(0, tiles)
        def _(t):
            at = pl.ds(pl.multiple_of(t * tile, tile), tile)
            anchor_cols[c, at, :] = anchor_cols[c, at, :] + cols[c, at, :] - product(at, ((0, kp, 0),), rhs2)

    def send_back(c):
        def source(peer):
            return anchor_cols.at[c, pl.ds(pl.multiple_of(peer * rows, rows), rows), :]

        @pl.loop(0, half)
        def _(step):
            peer = peer_of(step, True)
            send(source(peer), slab.at[c, me], b_send.at[c], b_recv.at[c], frame, peer)

            @pl.when(step > 0)
            def _():
                peer = peer_of(step, False)
                send(source(peer), slab.at[c, me], b_send.at[c], b_recv.at[c], frame, peer)

        pltpu.make_async_copy(source(me), slab.at[c, me], b_recv.at[c]).start()

        @pl.when(full_there)
        def _():
            @pl.loop(0, half)
            def _(step):
                peer = peer_of(step, True)
                send(source(peer), halo.at[c, core, me], h_send.at[c], h_recv.at[c], full_frame, peer)

    def send_halo(c):
        wait(slab.at[c], b_recv.at[c])

        @pl.when(full_there)
        def _():
            send(slab.at[c], halo.at[c, core], h_send.at[c], h_recv.at[c], full_frame, me)

        @pl.when(half_there)
        def _():
            some = pl.ds(z_lo * half, half)
            send(slab.at[c, some], halo.at[c, core, some], h_send.at[c], h_recv.at[c], half_frame, me)

        send(slab.at[c], part.at[c], p_send.at[c], p_recv.at[c], partner, me)

    @pl.loop(0, chunks)
    def _(c):
        transform(c)
        send_back(c)

        @pl.when(c > 0)
        def _():
            send_halo(c - 1)

    send_halo(chunks - 1)

    near, far = 1 - core, core

    def first_step(c):
        wait(part.at[c], p_recv.at[c])

        @pl.when(near_there)
        def _():
            wait(halo.at[c], h_recv.at[c])

        @pl.loop(0, slabs)
        def _(b):
            a, p = slab[c, b], part[c, b]
            x, y = halo[c, near, b], halo[c, far, b]
            across = jnp.where(near_there, flux(x - a), 0.0)
            own1[c, b] = a + step_size * tv_weight * (flux(p - a) + across)
            near1[c, b] = x + step_size * tv_weight * (flux(y - x) - across)

        send(own1.at[c], part1.at[c], q_send.at[c], q_recv.at[c], partner, me)

    def second_step(c):
        wait(part1.at[c], q_recv.at[c])

        @pl.loop(0, slabs)
        def _(b):
            a, u = slab[c, b], own1[c, b]
            across = jnp.where(near_there, flux(near1[c, b] - u), 0.0)
            result = u - step_size * ((u - a) - tv_weight * (flux(part1[c, b] - u) + across))
            out[0, :, pl.ds(pl.multiple_of(b * width + c * n, n), n)] = result

    @pl.loop(0, chunks)
    def _(c):
        first_step(c)

        @pl.when(c > 0)
        def _():
            second_step(c - 1)

    second_step(chunks - 1)

    @pl.loop(0, chunks)
    def _(c):
        wait(slab.at[c, pl.ds(0, slabs - 1)], f_send.at[c])
        wait(slab.at[c, pl.ds(0, slabs - 1)], b_send.at[c])
        wait(slab.at[c], p_send.at[c])
        wait(slab.at[c], q_send.at[c])

        @pl.when(full_there)
        def _():
            wait(slab.at[c], h_send.at[c])
            wait(slab.at[c, pl.ds(0, half)], h_send.at[c])

        @pl.when(half_there)
        def _():
            wait(slab.at[c, pl.ds(0, half)], h_send.at[c])


def on_device(volume, measured, cutoff):
    _, rows, pixels = volume.shape
    _, _, length, width = measured.shape
    slabs = pixels // width
    n = 128
    chunks = width // n
    most = 3 * length // 8
    kp = length // 2
    kr = -(-(most + 1) // 16) * 16
    upper = (length - most) // 128 * 128
    kranges = ((0, kp, 0), (upper, length, kp)) if upper >= kp else ((0, length, 0),)
    cfg = (length, slabs, rows, width, n, chunks, kr, kp, kranges)
    piece = (chunks, slabs, rows, n)
    dma = pltpu.SemaphoreType.DMA
    hbm = pl.BlockSpec(memory_space=pl.ANY)
    vmem = pl.BlockSpec(memory_space=pltpu.VMEM)
    return pl.pallas_call(
        functools.partial(kernel, cfg),
        out_shape=jax.ShapeDtypeStruct(volume.shape, F32),
        in_specs=[hbm, hbm, vmem, hbm, hbm, hbm, hbm],
        out_specs=vmem,
        scratch_shapes=[
            pltpu.VMEM((chunks, length, n), F32),
            pltpu.VMEM((chunks, length, n), F32),
            pltpu.VMEM((chunks, 2, length, n), F32),
            *[pltpu.VMEM((length, length), BF16)] * 4,
            pltpu.VMEM((2, length, 2 * n), BF16),
            pltpu.VMEM((2, kp, 2 * n), BF16),
            pltpu.VMEM(piece, F32),
            pltpu.VMEM((chunks, 2, slabs, rows, n), F32),
            *[pltpu.VMEM(piece, F32)] * 4,
            dma((4,)),
            *[dma((chunks,))] * 11,
        ],
        compiler_params=pltpu.CompilerParams(
            collective_id=0, has_side_effects=True, vmem_limit_bytes=60 * 1024 * 1024
        ),
        cost_estimate=pl.CostEstimate(flops=10**10, bytes_accessed=2**24, transcendentals=0),
    )(volume, measured, cutoff, *tables(length))


def solution(mesh):
    placed = (P("frame", "slab", None), P("frame", None, None, "slab"), P("frame", "slab"))
    return jax.shard_map(
        on_device, mesh=mesh, in_specs=placed, out_specs=P("frame", "slab", None), check_vma=False
    )
```

time: 415 us -> 138 us (0.33)
  the two profiles are of different devices: /device:TPU:65 before, /device:TPU:32 now
where the time goes in v1:
time: 138 us
  Pallas kernels  135 us (98%)
  local copies, waits for them, and re-layouts  3.05 us (2%)
    pallas_call x1, Pallas kernels, on_device(): pl.pallas_call(functools.partial(kernel, cfg), out_shape=jax.ShapeDtypeSt...  135 us
    unnamed x1, local copies, waits for them, and re-layouts  3.05 us

profile of v1, /device:TPU:32, one launch (start us, length us, event | category | flops | bytes accessed | tf_op | source)
XLA Modules:
  0.0 138.3 jit_solution(1500174468564352459)
XLA Ops:
  0.0 135.2 %shard_map.73 = f32[1,32,16384]{2,1,0:T(8,128)} custom-call(f32[1,32,16384]{2,1,0:T(8,128)} %volume.1, f32[1,2,1024,512]{3,2,1,0:T(8,128)} %measured.1, s32[1,512]{1,0:T(1,128)} %cutoff.1, bf16[1024,1024]{1,0:T(8,128)(2,1)} %constant.8.clone.ch_hbm, bf16[1024,1024]{1,0:T(8,128)(2,1)} %constant.9.clone.cl_hbm, bf16[1024,1024]{1,0:T(8,128)(2,1)} %constant.10.clone.sh_hbm, ...), custom_call_target="tpu_custom_call" | custom-call | flops 10000000000 | bytes 16777216 | tf_op jit(solution)/shard_map/pallas_call | solution.py:315
  135.2 3.0 %copy.9 = f32[1,32,16384]{2,1,0:T(8,128)} copy(f32[1,32,16384]{2,1,0:T(8,128)} %shard_map.73) | data formatting | bytes 4194304

commit v2 on v1

--- a/solution.py
+++ b/solution.py
@@ -47,6 +47,7 @@
 ):
     length, slabs, rows, width, n, chunks, kr, kp, kranges = cfg
     half = slabs // 2
+    ahead = min(2, chunks)
     frame, me = lax.axis_index("frame"), lax.axis_index("slab")
     frames = lax.axis_size("frame")
     block, core = lax.div(frame, 2), lax.rem(frame, 2)
@@ -119,8 +120,7 @@
     )
     pl.semaphore_wait(barrier, expected)
 
-    @pl.loop(0, chunks)
-    def _(c):
+    def send_columns(c):
         def source(peer):
             return volume.at[0, :, pl.ds(pl.multiple_of(peer * width + c * n, n), n)]
 
@@ -137,6 +137,10 @@
                 send(source(peer), target, f_send.at[c], f_recv.at[c], frame, peer)
 
         pltpu.make_async_copy(source(me), target, f_recv.at[c]).start()
+
+    @pl.loop(0, ahead)
+    def _(c):
+        send_columns(c)
 
     for copy in local[:4]:
         copy.wait()
@@ -174,6 +178,11 @@
             anchor_cols[c, at, :] = product(at, kranges, rhs)
 
         wait(cols.at[c], f_recv.at[c])
+
+        @pl.when(c + ahead < chunks)
+        def _():
+            send_columns(c + ahead)
+
         head, rest = split(cols[c])
         rhs[0, 0:length, :n] = head
         rhs[0, 0:length, n:] = rest
@@ -213,21 +222,27 @@
             @pl.loop(0, half)
             def _(step):
                 peer = peer_of(step, True)
-                send(source(peer), halo.at[c, core, me], h_send.at[c], h_recv.at[c], full_frame, peer)
+                send(source(peer), halo.at[c, core, me], h_send.at[c], h_recv.at[c, z_lo], full_frame, peer)
 
     def send_halo(c):
         wait(slab.at[c], b_recv.at[c])
 
-        @pl.when(full_there)
-        def _():
-            send(slab.at[c], halo.at[c, core], h_send.at[c], h_recv.at[c], full_frame, me)
-
-        @pl.when(half_there)
-        def _():
-            some = pl.ds(z_lo * half, half)
-            send(slab.at[c, some], halo.at[c, core, some], h_send.at[c], h_recv.at[c], half_frame, me)
-
-        send(slab.at[c], part.at[c], p_send.at[c], p_recv.at[c], partner, me)
+        for h in (z_lo, 1 - z_lo):
+            some = pl.ds(h * half, half)
+
+            @pl.when(full_there)
+            def _():
+                send(slab.at[c, some], halo.at[c, core, some], h_send.at[c], h_recv.at[c, h], full_frame, me)
+
+            if h is z_lo:
+
+                @pl.when(half_there)
+                def _():
+                    send(slab.at[c, some], halo.at[c, core, some], h_send.at[c], h_recv.at[c, h], half_frame, me)
+
+        for h in (1 - core, core):
+            some = pl.ds(h * half, half)
+            send(slab.at[c, some], part.at[c, some], p_send.at[c], p_recv.at[c, h], partner, me)
 
     @pl.loop(0, chunks)
     def _(c):
@@ -242,28 +257,31 @@
 
     near, far = 1 - core, core
 
-    def first_step(c):
-        wait(part.at[c], p_recv.at[c])
+    def first_step(c, h):
+        some = pl.ds(h * half, half)
+        wait(part.at[c, some], p_recv.at[c, h])
 
         @pl.when(near_there)
         def _():
-            wait(halo.at[c], h_recv.at[c])
-
-        @pl.loop(0, slabs)
-        def _(b):
+            wait(halo.at[c, 0], h_recv.at[c, h])
+
+        @pl.loop(0, half)
+        def _(i):
+            b = h * half + i
             a, p = slab[c, b], part[c, b]
             x, y = halo[c, near, b], halo[c, far, b]
             across = jnp.where(near_there, flux(x - a), 0.0)
             own1[c, b] = a + step_size * tv_weight * (flux(p - a) + across)
             near1[c, b] = x + step_size * tv_weight * (flux(y - x) - across)
 
-        send(own1.at[c], part1.at[c], q_send.at[c], q_recv.at[c], partner, me)
-
-    def second_step(c):
-        wait(part1.at[c], q_recv.at[c])
-
-        @pl.loop(0, slabs)
-        def _(b):
+        send(own1.at[c, some], part1.at[c, some], q_send.at[c], q_recv.at[c, h], partner, me)
+
+    def second_step(c, h):
+        wait(part1.at[c, pl.ds(h * half, half)], q_recv.at[c, h])
+
+        @pl.loop(0, half)
+        def _(i):
+            b = h * half + i
             a, u = slab[c, b], own1[c, b]
             across = jnp.where(near_there, flux(near1[c, b] - u), 0.0)
             result = u - step_size * ((u - a) - tv_weight * (flux(part1[c, b] - u) + across))
@@ -271,13 +289,16 @@
 
     @pl.loop(0, chunks)
     def _(c):
-        first_step(c)
+        first_step(c, 1 - core)
 
         @pl.when(c > 0)
         def _():
-            second_step(c - 1)
-
-    second_step(chunks - 1)
+            second_step(c - 1, core)
+
+        first_step(c, core)
+        second_step(c, 1 - core)
+
+    second_step(chunks - 1, core)
 
     @pl.loop(0, chunks)
     def _(c):
@@ -314,7 +335,7 @@
     vmem = pl.BlockSpec(memory_space=pltpu.VMEM)
     return pl.pallas_call(
         functools.partial(kernel, cfg),
-        out_shape=jax.ShapeDtypeStruct(volume.shape, F32),
+        out_shape=pltpu.VMEM(volume.shape, F32),
         in_specs=[hbm, hbm, vmem, hbm, hbm, hbm, hbm],
         out_specs=vmem,
         scratch_shapes=[
@@ -328,7 +349,8 @@
             pltpu.VMEM((chunks, 2, slabs, rows, n), F32),
             *[pltpu.VMEM(piece, F32)] * 4,
             dma((4,)),
-            *[dma((chunks,))] * 11,
+            *[dma((chunks,))] * 5,
+            *[dma((chunks,)), dma((chunks, 2))] * 3,
         ],
         compiler_params=pltpu.CompilerParams(
             collective_id=0, has_side_effects=True, vmem_limit_bytes=60 * 1024 * 1024

time: 138 us -> 132 us (0.957)
  Pallas kernels: 135 us -> 130 us
  local copies, waits for them, and re-layouts: 3.05 us -> 1.32 us
    pallas_call x1, Pallas kernels: 135 us -> 130 us  [on_device(): pl.pallas_call(functools.partial(kernel, cfg), out_shape=pltpu.VMEM(volum...]
    unnamed x1, local copies, waits for them, and re-layouts: 3.05 us -> 1.32 us
where the time goes in v2:
time: 132 us
  Pallas kernels  130 us (98%)
  local copies, waits for them, and re-layouts  1.32 us (1%)
    pallas_call x1, Pallas kernels, on_device(): pl.pallas_call(functools.partial(kernel, cfg), out_shape=pltpu.VMEM(volum...  130 us

profile of v2, /device:TPU:32, one launch (start us, length us, event | category | flops | bytes accessed | tf_op | source)
XLA Modules:
  0.0 131.5 jit_solution(9515970312572010864)
XLA Ops:
  0.0 130.2 %shard_map.73 = f32[1,32,16384]{2,1,0:T(8,128)S(1)} custom-call(f32[1,32,16384]{2,1,0:T(8,128)} %volume.1, f32[1,2,1024,512]{3,2,1,0:T(8,128)} %measured.1, s32[1,512]{1,0:T(1,128)} %cutoff.1, bf16[1024,1024]{1,0:T(8,128)(2,1)} %constant.8.clone.ch_hbm, bf16[1024,1024]{1,0:T(8,128)(2,1)} %constant.9.clone.cl_hbm, bf16[1024,1024]{1,0:T(8,128)(2,1)} %constant.10.clone.sh_hbm, ...), custom_call_target="tpu_custom_call" | custom-call | flops 10000000000 | bytes 16777216 | tf_op jit(solution)/shard_map/pallas_call | solution.py:336
  130.2 1.3 %copy.9 = f32[1,32,16384]{2,1,0:T(8,128)} copy(f32[1,32,16384]{2,1,0:T(8,128)S(1)} %shard_map.73) | data formatting | bytes 4194304

commit v3 on v2

--- a/solution.py
+++ b/solution.py
@@ -48,6 +48,7 @@
     length, slabs, rows, width, n, chunks, kr, kp, kranges = cfg
     half = slabs // 2
     ahead = min(2, chunks)
+    unroll = min(4, half)
     frame, me = lax.axis_index("frame"), lax.axis_index("slab")
     frames = lax.axis_size("frame")
     block, core = lax.div(frame, 2), lax.rem(frame, 2)
@@ -70,12 +71,18 @@
     def wait(like, sem):
         pltpu.make_async_copy(like, like, sem).wait()
 
-    def peer_of(step, across):
-        if half == 16:
-            there = lax.rem(lax.div(place, 4) + lax.div(step, 4), 4) * 4 + lax.rem(place + step, 4)
-        else:
-            there = lax.rem(place + step, half)
-        return (1 - z_lo if across else z_lo) * half + there
+    wide = 4 if half == 16 else 1
+    deep = half // wide
+    x, y = lax.div(place, deep), lax.rem(place, deep)
+    ys = [lax.rem(y + j, deep) for j in range(deep)]
+    same, other = z_lo * half, (1 - z_lo) * half
+
+    def each_peer(act):
+        @pl.loop(0, wide)
+        def _(i):
+            row = lax.rem(x + i, wide) * deep
+            for j in range(deep):
+                act(row + ys[j], (i == 0) if j == 0 else False)
 
     local = [
         pltpu.make_async_copy(src, dst, local_sem.at[i])
@@ -93,18 +100,25 @@
     def greet(to_frame, to_slab):
         pl.semaphore_signal(barrier, inc=1, device_id=(to_frame, to_slab), device_id_type=MESH)
 
-    @pl.loop(0, half)
-    def _(step):
-        greet(frame, peer_of(step, True))
-
-        @pl.when(step > 0)
-        def _():
-            greet(frame, peer_of(step, False))
-
-        @pl.when(near_there & (z_lo == core))
-        def _():
-            greet(2 * near_block, peer_of(step, True))
-            greet(2 * near_block + 1, peer_of(step, True))
+    def unless(own, act):
+        if own is False:
+            act()
+        else:
+            pl.when(jnp.logical_not(own))(act)
+
+    def greet_group(at, own):
+        greet(frame, other + at)
+        unless(own, lambda: greet(frame, same + at))
+
+    def greet_near(at, own):
+        greet(2 * near_block, other + at)
+        greet(2 * near_block + 1, other + at)
+
+    each_peer(greet_group)
+
+    @pl.when(near_there & (z_lo == core))
+    def _():
+        each_peer(greet_near)
 
     greet(partner, me)
 
@@ -126,19 +140,17 @@
 
         target = cols.at[c, pl.ds(pl.multiple_of(me * rows, rows), rows), :]
 
-        @pl.loop(0, half)
-        def _(step):
-            peer = peer_of(step, True)
+        def give(peer):
             send(source(peer), target, f_send.at[c], f_recv.at[c], frame, peer)
 
-            @pl.when(step > 0)
-            def _():
-                peer = peer_of(step, False)
-                send(source(peer), target, f_send.at[c], f_recv.at[c], frame, peer)
-
+        def both(at, own):
+            give(other + at)
+            unless(own, lambda: give(same + at))
+
+        each_peer(both)
         pltpu.make_async_copy(source(me), target, f_recv.at[c]).start()
 
-    @pl.loop(0, ahead)
+    @pl.loop(0, min(3, chunks))
     def _(c):
         send_columns(c)
 
@@ -161,8 +173,11 @@
                 narrow = second if narrow is None else narrow + second
         return wide[:, :n] + wide[:, n:] + narrow
 
-    def transform(c):
-        limit = cutoff[0:1, pl.ds(pl.multiple_of(c * n, n), n)]
+    def limits(c):
+        return cutoff[0:1, pl.ds(pl.multiple_of(c * n, n), n)]
+
+    def transform_measured(c):
+        limit = limits(c)
         wait(meas.at[c], meas_sem.at[c])
         for low, high, base in kranges:
             k = lax.broadcasted_iota(jnp.int32, (high - low, n), 0) + low
@@ -177,17 +192,13 @@
             at = pl.ds(pl.multiple_of(t * tile, tile), tile)
             anchor_cols[c, at, :] = product(at, kranges, rhs)
 
+    def transform_volume(c):
         wait(cols.at[c], f_recv.at[c])
-
-        @pl.when(c + ahead < chunks)
-        def _():
-            send_columns(c + ahead)
-
         head, rest = split(cols[c])
         rhs[0, 0:length, :n] = head
         rhs[0, 0:length, n:] = rest
         k = lax.broadcasted_iota(jnp.int32, (kr, n), 0)
-        weight = jnp.where(k <= limit, jnp.where(k == 0, 1.0, 2.0), 0.0)
+        weight = jnp.where(k <= limits(c), jnp.where(k == 0, 1.0, 2.0), 0.0)
         for i, (head, rest) in enumerate(((ch, cl), (sh, sl))):
             both = rhs[0, 0:length, :]
             wide = jnp.dot(head[:kr, :], both, preferred_element_type=F32)
@@ -205,55 +216,64 @@
         def source(peer):
             return anchor_cols.at[c, pl.ds(pl.multiple_of(peer * rows, rows), rows), :]
 
-        @pl.loop(0, half)
-        def _(step):
-            peer = peer_of(step, True)
-            send(source(peer), slab.at[c, me], b_send.at[c], b_recv.at[c], frame, peer)
-
-            @pl.when(step > 0)
+        def give(peer):
+            send(source(peer), slab.at[c, me], b_send.at[c], b_recv.at[c, z_lo], frame, peer)
+
+        def both(at, own):
+            give(other + at)
+            unless(own, lambda: give(same + at))
+
+        each_peer(both)
+        pltpu.make_async_copy(source(me), slab.at[c, me], b_recv.at[c, z_lo]).start()
+
+        @pl.when(full_there)
+        def _():
+            each_peer(
+                lambda at, own: send(
+                    source(other + at), halo.at[c, core, me], h_send.at[c], h_recv.at[c, z_lo], full_frame, other + at
+                )
+            )
+
+    def send_halo(c, h):
+        some = pl.ds(h * half, half)
+        wait(slab.at[c, some], b_recv.at[c, h])
+
+        @pl.when(full_there)
+        def _():
+            send(slab.at[c, some], halo.at[c, core, some], h_send.at[c], h_recv.at[c, h], full_frame, me)
+
+        if h is z_lo:
+
+            @pl.when(half_there)
             def _():
-                peer = peer_of(step, False)
-                send(source(peer), slab.at[c, me], b_send.at[c], b_recv.at[c], frame, peer)
-
-        pltpu.make_async_copy(source(me), slab.at[c, me], b_recv.at[c]).start()
-
-        @pl.when(full_there)
-        def _():
-            @pl.loop(0, half)
-            def _(step):
-                peer = peer_of(step, True)
-                send(source(peer), halo.at[c, core, me], h_send.at[c], h_recv.at[c, z_lo], full_frame, peer)
-
-    def send_halo(c):
-        wait(slab.at[c], b_recv.at[c])
-
-        for h in (z_lo, 1 - z_lo):
-            some = pl.ds(h * half, half)
-
-            @pl.when(full_there)
-            def _():
-                send(slab.at[c, some], halo.at[c, core, some], h_send.at[c], h_recv.at[c, h], full_frame, me)
-
-            if h is z_lo:
-
-                @pl.when(half_there)
-                def _():
-                    send(slab.at[c, some], halo.at[c, core, some], h_send.at[c], h_recv.at[c, h], half_frame, me)
-
-        for h in (1 - core, core):
-            some = pl.ds(h * half, half)
-            send(slab.at[c, some], part.at[c, some], p_send.at[c], p_recv.at[c, h], partner, me)
+                send(slab.at[c, some], halo.at[c, core, some], h_send.at[c], h_recv.at[c, h], half_frame, me)
+
+        send(slab.at[c, some], part.at[c, some], p_send.at[c], p_recv.at[c, h], partner, me)
+
+    @pl.loop(0, ahead)
+    def _(c):
+        transform_measured(c)
 
     @pl.loop(0, chunks)
     def _(c):
-        transform(c)
+        transform_volume(c)
         send_back(c)
 
+        @pl.when(c + 3 < chunks)
+        def _():
+            send_columns(c + 3)
+
+        @pl.when(c + ahead < chunks)
+        def _():
+            transform_measured(c + ahead)
+
         @pl.when(c > 0)
         def _():
-            send_halo(c - 1)
-
-    send_halo(chunks - 1)
+            send_halo(c - 1, z_lo)
+            send_halo(c - 1, 1 - z_lo)
+
+    send_halo(chunks - 1, z_lo)
+    send_halo(chunks - 1, 1 - z_lo)
 
     near, far = 1 - core, core
 
@@ -265,21 +285,26 @@
         def _():
             wait(halo.at[c, 0], h_recv.at[c, h])
 
-        @pl.loop(0, half)
+        @pl.loop(0, half, unroll=unroll)
         def _(i):
             b = h * half + i
-            a, p = slab[c, b], part[c, b]
-            x, y = halo[c, near, b], halo[c, far, b]
-            across = jnp.where(near_there, flux(x - a), 0.0)
-            own1[c, b] = a + step_size * tv_weight * (flux(p - a) + across)
-            near1[c, b] = x + step_size * tv_weight * (flux(y - x) - across)
+            a = slab[c, b]
+            across = jnp.where(near_there, flux(halo[c, near, b] - a), 0.0)
+            own1[c, b] = a + step_size * tv_weight * (flux(part[c, b] - a) + across)
+            near1[c, b] = across
 
         send(own1.at[c, some], part1.at[c, some], q_send.at[c], q_recv.at[c, h], partner, me)
+
+        @pl.loop(0, half, unroll=unroll)
+        def _(i):
+            b = h * half + i
+            x = halo[c, near, b]
+            near1[c, b] = x + step_size * tv_weight * (flux(halo[c, far, b] - x) - near1[c, b])
 
     def second_step(c, h):
         wait(part1.at[c, pl.ds(h * half, half)], q_recv.at[c, h])
 
-        @pl.loop(0, half)
+        @pl.loop(0, half, unroll=unroll)
         def _(i):
             b = h * half + i
             a, u = slab[c, b], own1[c, b]
@@ -349,8 +374,8 @@
             pltpu.VMEM((chunks, 2, slabs, rows, n), F32),
             *[pltpu.VMEM(piece, F32)] * 4,
             dma((4,)),
-            *[dma((chunks,))] * 5,
-            *[dma((chunks,)), dma((chunks, 2))] * 3,
+            *[dma((chunks,))] * 3,
+            *[dma((chunks,)), dma((chunks, 2))] * 4,
         ],
         compiler_params=pltpu.CompilerParams(
             collective_id=0, has_side_effects=True, vmem_limit_bytes=60 * 1024 * 1024

time: 132 us -> 131 us (level)
  no operation moved by 1% of the time
where the time goes in v3:
time: 131 us
  Pallas kernels  129 us (98%)
  local copies, waits for them, and re-layouts  1.32 us (1%)
    pallas_call x1, Pallas kernels, on_device(): pl.pallas_call(functools.partial(kernel, cfg), out_shape=pltpu.VMEM(volum...  129 us

profile of v3, /device:TPU:32, one launch (start us, length us, event | category | flops | bytes accessed | tf_op | source)
XLA Modules:
  0.0 130.7 jit_solution(7859208570602711881)
XLA Ops:
  0.0 129.3 %shard_map.73 = f32[1,32,16384]{2,1,0:T(8,128)S(1)} custom-call(f32[1,32,16384]{2,1,0:T(8,128)} %volume.1, f32[1,2,1024,512]{3,2,1,0:T(8,128)} %measured.1, s32[1,512]{1,0:T(1,128)} %cutoff.1, bf16[1024,1024]{1,0:T(8,128)(2,1)} %constant.8.clone.ch_hbm, bf16[1024,1024]{1,0:T(8,128)(2,1)} %constant.9.clone.cl_hbm, bf16[1024,1024]{1,0:T(8,128)(2,1)} %constant.10.clone.sh_hbm, ...), custom_call_target="tpu_custom_call" | custom-call | flops 10000000000 | bytes 16777216 | tf_op jit(solution)/shard_map/pallas_call | solution.py:361
  129.3 1.3 %copy.9 = f32[1,32,16384]{2,1,0:T(8,128)} copy(f32[1,32,16384]{2,1,0:T(8,128)S(1)} %shard_map.73) | data formatting | bytes 4194304

commit v4 on v3

--- a/solution.py
+++ b/solution.py
@@ -173,6 +173,8 @@
                 narrow = second if narrow is None else narrow + second
         return wide[:, :n] + wide[:, n:] + narrow
 
+    edge = (block == 0) | (block == blocks - 1)
+
     def limits(c):
         return cutoff[0:1, pl.ds(pl.multiple_of(c * n, n), n)]
 
@@ -267,13 +269,17 @@
         def _():
             transform_measured(c + ahead)
 
-        @pl.when(c > 0)
-        def _():
-            send_halo(c - 1, z_lo)
-            send_halo(c - 1, 1 - z_lo)
-
-    send_halo(chunks - 1, z_lo)
-    send_halo(chunks - 1, 1 - z_lo)
+        late = jnp.where(edge, 0, 1)
+
+        @pl.when(c >= late)
+        def _():
+            send_halo(c - late, z_lo)
+            send_halo(c - late, 1 - z_lo)
+
+    @pl.when(jnp.logical_not(edge))
+    def _():
+        send_halo(chunks - 1, z_lo)
+        send_halo(chunks - 1, 1 - z_lo)
 
     near, far = 1 - core, core
 

time: 131 us -> 130 us (level)
  no operation moved by 1% of the time
where the time goes in v4:
time: 130 us
  Pallas kernels  128 us (98%)
  local copies, waits for them, and re-layouts  1.32 us (1%)
    pallas_call x1, Pallas kernels, on_device(): pl.pallas_call(functools.partial(kernel, cfg), out_shape=pltpu.VMEM(volum...  128 us

profile of v4, /device:TPU:32, one launch (start us, length us, event | category | flops | bytes accessed | tf_op | source)
XLA Modules:
  0.0 129.8 jit_solution(11131021367754457492)
XLA Ops:
  0.0 128.5 %shard_map.73 = f32[1,32,16384]{2,1,0:T(8,128)S(1)} custom-call(f32[1,32,16384]{2,1,0:T(8,128)} %volume.1, f32[1,2,1024,512]{3,2,1,0:T(8,128)} %measured.1, s32[1,512]{1,0:T(1,128)} %cutoff.1, bf16[1024,1024]{1,0:T(8,128)(2,1)} %constant.8.clone.ch_hbm, bf16[1024,1024]{1,0:T(8,128)(2,1)} %constant.9.clone.cl_hbm, bf16[1024,1024]{1,0:T(8,128)(2,1)} %constant.10.clone.sh_hbm, ...), custom_call_target="tpu_custom_call" | custom-call | flops 10000000000 | bytes 16777216 | tf_op jit(solution)/shard_map/pallas_call | solution.py:367
  128.5 1.3 %copy.9 = f32[1,32,16384]{2,1,0:T(8,128)} copy(f32[1,32,16384]{2,1,0:T(8,128)S(1)} %shard_map.73) | data formatting | bytes 4194304
